TPU v7x, 512 devices: a whole 4x4x16 slice. The times are simulated.
512 devices in a mesh: dp: 512 (over x, y, z, core).
Axes of the slice: x: 4, y: 4, z: 16, core: 2. Of those that a mesh axis runs over, the one named last changes fastest.
Arguments:
- image_embed: bfloat16 [262144, 768], P('dp'), may hold values from -1.5 to 1.5
- text_embed: bfloat16 [262144, 768], P('dp'), may hold values from -1.5 to 1.5
- logit_scale: float32 [1], replicated, may hold values from 1 to 3
- logit_bias: float32 [1], replicated, may hold values from -3 to 0
Outputs:
- row_loss: float32 [262144], P('dp')
- grad_image: float32 [262144, 768], P('dp')
- grad_text: float32 [262144, 768], P('dp')
All inputs are finite; a program needn't handle non-finite values.
Results may differ from a plain program's by a relative error of at most 0.0022.
Values may be sent and summed in bfloat16 or wider, within the bound.
A program may use at most 64 MiB of HBM per device.

v0:
```python
import jax
import jax.numpy as jnp
from jax import lax
from jax.sharding import PartitionSpec as P


def from_behind(block, axis, distance):
    devices = range(lax.axis_size(axis))
    route = [((i - distance) % len(devices), i) for i in devices]
    return lax.ppermute(block, axis, route)


def score_block(images, texts, scale, bias, labels):
    inner = jnp.dot(images, texts.T, preferred_element_type=jnp.float32)
    logits = scale * inner + bias
    losses = jnp.sum(jax.nn.softplus(-labels * logits), axis=1)
    positive = (labels > 0.0).astype(jnp.float32)
    coeff = (scale * (jax.nn.sigmoid(logits) - positive)).astype(jnp.bfloat16)
    grad_rows = jnp.dot(coeff, texts, preferred_element_type=jnp.float32)
    partial_cols = jnp.dot(coeff.T, images, preferred_element_type=jnp.float32)
    return (losses, grad_rows, partial_cols)


def body(image_embed, text_embed, logit_scale, logit_bias):
    rows_here = image_embed.shape[0]
    scale = logit_scale[0]
    bias = logit_bias[0]
    eye = jnp.eye(rows_here, dtype=jnp.float32)
    own_labels = 2.0 * eye - 1.0
    other_labels = -jnp.ones((rows_here, rows_here), jnp.float32)
    text_near = from_behind(text_embed, "dp", 1)
    text_second = from_behind(text_near, "dp", 1)
    loss_a, grad_a, part_own = score_block(image_embed, text_embed, scale, bias, own_labels)
    loss_b, grad_b, part_near = score_block(image_embed, text_near, scale, bias, other_labels)
    loss_c, grad_c, part_far = score_block(image_embed, text_second, scale, bias, other_labels)
    row_loss = (loss_a + loss_b + loss_c) / (3.0 * rows_here)
    grad_image = grad_a + grad_b + grad_c
    carried = from_behind(part_far, "dp", -1)
    returned = from_behind(part_near + carried, "dp", -1)
    grad_text = part_own + returned
    return (row_loss, grad_image, grad_text)


def solution(mesh):
    in_specs = (P("dp", None), P("dp", None), P(), P())
    out_specs = (P("dp"), P("dp", None), P("dp", None))
    return jax.shard_map(body, mesh=mesh, in_specs=in_specs, out_specs=out_specs, check_vma=False)
```

profile of v0, /device:TPU:6, one launch (start us, length us, event | category | flops | bytes accessed | tf_op | source)
XLA Modules:
  0.0 91.4 jit_solution(14488767624347080709)
XLA Ops:
  0.6 0.0 copy-start
  0.6 2.1 %collective-permute-start = (bf16[512,768]{1,0:T(8,128)(2,1)}, bf16[512,768]{1,0:T(8,128)(2,1)S(1)}, u32[]{:S(2)}, u32[]{:S(2)}) collective-permute-start(bf16[512,768]{1,0:T(8,128)(2,1)} %param.5), channel_id=1, source_target_pairs={{511,0},{0,1},{1,2},{2,3},{3,4},{4,5},{5,6},{6,7},{7,8},{8,9},{9,1... | collective-permute-start | bytes 2359304 | tf_op jit(solution)/shard_map/ppermute | solution.py:10
  2.7 21.5 %collective-permute-done = bf16[512,768]{1,0:T(8,128)(2,1)S(1)} collective-permute-done((bf16[512,768]{1,0:T(8,128)(2,1)}, bf16[512,768]{1,0:T(8,128)(2,1)S(1)}, u32[]{:S(2)}, u32[]{:S(2)}) %collective-permute-start) | collective-permute-done | bytes 786464 | tf_op jit(solution)/shard_map/ppermute | solution.py:10
  24.2 1.9 %collective-permute-start.1 = (bf16[512,768]{1,0:T(8,128)(2,1)S(1)}, bf16[512,768]{1,0:T(8,128)(2,1)S(1)}, u32[]{:S(2)}, u32[]{:S(2)}) collective-permute-start(bf16[512,768]{1,0:T(8,128)(2,1)S(1)} %collective-permute-done), channel_id=1, source_target_pairs={{511,0},{0,1},{1,2},{2,3},{3,4},{4,5},{5,6},{6,7},{7,8},{8,9},{9,1... | collective-permute-start | bytes 2359304 | tf_op jit(solution)/shard_map/ppermute | solution.py:10
  27.4 14.3 %collective-permute-done.1 = bf16[512,768]{1,0:T(8,128)(2,1)S(1)} collective-permute-done((bf16[512,768]{1,0:T(8,128)(2,1)S(1)}, bf16[512,768]{1,0:T(8,128)(2,1)S(1)}, u32[]{:S(2)}, u32[]{:S(2)}) %collective-permute-start.1) | collective-permute-done | bytes 786464 | tf_op jit(solution)/shard_map/ppermute | solution.py:10
  41.7 0.0 copy-done
  41.7 1.1 %fusion.5 = (f32[512]{0:T(512)S(1)}, f32[512,512]{0,1:T(8,128)S(1)}) fusion(f32[]{:T(128)} %bitcast.24, bf16[512,768]{1,0:T(8,128)(2,1)S(1)} %copy-done, bf16[512,768]{1,0:T(8,128)(2,1)S(1)} %collective-permute-done.1, f32[]{:T(128)} %bitcast.18), kind=kOutput, calls=%fused_computation.13 | convolution fusion | flops 405011968 | bytes 2623496 | tf_op jit(solution)/shard_map/dot_general | solution.py:14
  42.9 0.0 copy-start.1
  42.9 0.7 fusion.8
  43.6 1.9 %collective-permute-start.2 = (f32[512,768]{1,0:T(8,128)S(1)}, f32[512,768]{1,0:T(8,128)S(1)}, u32[]{:S(2)}, u32[]{:S(2)}) collective-permute-start(f32[512,768]{1,0:T(8,128)S(1)} %fusion.8), channel_id=1, source_target_pairs={{1,0},{2,1},{3,2},{4,3},{5,4},{6,5},{7,6},{8,7},{9,8},{10,9},{11,1... | collective-permute-start | bytes 4718600 | tf_op jit(solution)/shard_map/ppermute | solution.py:10
  45.5 0.0 copy-done.1
  45.5 1.2 %fusion.3 = (f32[512]{0:T(512)S(1)}, f32[512,512]{0,1:T(8,128)S(1)}) fusion(f32[]{:T(128)} %bitcast.23, bf16[512,768]{1,0:T(8,128)(2,1)S(1)} %copy-done, bf16[512,768]{1,0:T(8,128)(2,1)S(1)} %copy-done.1, f32[]{:T(128)} %bitcast.14), kind=kOutput, calls=%fused_computation.11 | convolution fusion | flops 406322688 | bytes 2623496 | tf_op jit(solution)/shard_map/dot_general | solution.py:14
  46.7 1.1 %fusion.4 = (f32[512]{0:T(512)S(1)}, f32[512,512]{0,1:T(8,128)S(1)}) fusion(f32[]{:T(128)} %bitcast.25, bf16[512,768]{1,0:T(8,128)(2,1)S(1)} %copy-done, bf16[512,768]{1,0:T(8,128)(2,1)S(1)} %collective-permute-done, f32[]{:T(128)} %bitcast.19), kind=kOutput, calls=%fused_computation.12 | convolution fusion | flops 405011968 | bytes 2623496 | tf_op jit(solution)/shard_map/dot_general | solution.py:14
  47.9 15.6 %collective-permute-done.2 = f32[512,768]{1,0:T(8,128)S(1)} collective-permute-done((f32[512,768]{1,0:T(8,128)S(1)}, f32[512,768]{1,0:T(8,128)S(1)}, u32[]{:S(2)}, u32[]{:S(2)}) %collective-permute-start.2) | collective-permute-done | bytes 1572896 | tf_op jit(solution)/shard_map/ppermute | solution.py:10
  63.4 0.7 convolution_add_fusion
  64.1 8.0 %collective-permute-start.3 = (f32[512,768]{1,0:T(8,128)S(1)}, f32[512,768]{1,0:T(8,128)S(1)}, u32[]{:S(2)}, u32[]{:S(2)}) collective-permute-start(f32[512,768]{1,0:T(8,128)S(1)} %convolution_add_fusion), channel_id=1, source_target_pairs={{1,0},{2,1},{3,2},{4,3},{5,4},{6,5},{7,6},{8,7},{9,8},{10,9},{11,1... | collective-permute-start | bytes 4718600 | tf_op jit(solution)/shard_map/ppermute | solution.py:10
  72.2 0.7 fusion.9
  72.9 0.7 fusion.10
  73.6 0.6 fusion.7
  74.2 0.6 add_multiply_fusion
  74.8 1.8 %add_add_fusion = f32[512,768]{1,0:T(8,128)} fusion(f32[512,768]{1,0:T(8,128)S(1)} %fusion.10, f32[512,768]{1,0:T(8,128)S(1)} %fusion.7, bf16[512,768]{1,0:T(8,128)(2,1)S(1)} %collective-permute-done.1, f32[512,512]{0,1:T(8,128)S(1)} %get-tuple-element.4, f32[]{:T(128)} %bitcast.15), kind=kOutput, calls=%fused_computation.3 | convolution fusion | flops 404750336 | bytes 6553604 | tf_op jit(solution)/shard_map/dot_general | solution.py:19
  76.6 13.5 %collective-permute-done.3 = f32[512,768]{1,0:T(8,128)S(1)} collective-permute-done((f32[512,768]{1,0:T(8,128)S(1)}, f32[512,768]{1,0:T(8,128)S(1)}, u32[]{:S(2)}, u32[]{:S(2)}) %collective-permute-start.3) | collective-permute-done | bytes 1572896 | tf_op jit(solution)/shard_map/ppermute | solution.py:10
  90.1 1.3 %add.67 = f32[512,768]{1,0:T(8,128)} add(f32[512,768]{1,0:T(8,128)S(1)} %fusion.9, f32[512,768]{1,0:T(8,128)S(1)} %collective-permute-done.3) | non-fusion elementwise | flops 393216 | bytes 4718592 | tf_op jit(solution)/shard_map/add | solution.py:40
Async XLA Ops:
  0.6 41.1 %copy-start = (bf16[512,768]{1,0:T(8,128)(2,1)S(1)}, bf16[512,768]{1,0:T(8,128)(2,1)}, u32[]{:S(2)}) copy-start(bf16[512,768]{1,0:T(8,128)(2,1)} %param.4) | copy-start | bytes 2359300
  0.6 23.6 %collective-permute-start = (bf16[512,768]{1,0:T(8,128)(2,1)}, bf16[512,768]{1,0:T(8,128)(2,1)S(1)}, u32[]{:S(2)}, u32[]{:S(2)}) collective-permute-start(bf16[512,768]{1,0:T(8,128)(2,1)} %param.5), channel_id=1, source_target_pairs={{511,0},{0,1},{1,2},{2,3},{3,4},{4,5},{5,6},{6,7},{7,8},{8,9},{9,1... | collective-permute-start | bytes 2359304 | tf_op jit(solution)/shard_map/ppermute | solution.py:10
  24.2 17.5 %collective-permute-start.1 = (bf16[512,768]{1,0:T(8,128)(2,1)S(1)}, bf16[512,768]{1,0:T(8,128)(2,1)S(1)}, u32[]{:S(2)}, u32[]{:S(2)}) collective-permute-start(bf16[512,768]{1,0:T(8,128)(2,1)S(1)} %collective-permute-done), channel_id=1, source_target_pairs={{511,0},{0,1},{1,2},{2,3},{3,4},{4,5},{5,6},{6,7},{7,8},{8,9},{9,1... | collective-permute-start | bytes 2359304 | tf_op jit(solution)/shard_map/ppermute | solution.py:10
  42.9 2.7 %copy-start.1 = (bf16[512,768]{1,0:T(8,128)(2,1)S(1)}, bf16[512,768]{1,0:T(8,128)(2,1)}, u32[]{:S(2)}) copy-start(bf16[512,768]{1,0:T(8,128)(2,1)} %param.5) | copy-start | bytes 2359300
  43.6 19.8 %collective-permute-start.2 = (f32[512,768]{1,0:T(8,128)S(1)}, f32[512,768]{1,0:T(8,128)S(1)}, u32[]{:S(2)}, u32[]{:S(2)}) collective-permute-start(f32[512,768]{1,0:T(8,128)S(1)} %fusion.8), channel_id=1, source_target_pairs={{1,0},{2,1},{3,2},{4,3},{5,4},{6,5},{7,6},{8,7},{9,8},{10,9},{11,1... | collective-permute-start | bytes 4718600 | tf_op jit(solution)/shard_map/ppermute | solution.py:10
  64.1 26.0 %collective-permute-start.3 = (f32[512,768]{1,0:T(8,128)S(1)}, f32[512,768]{1,0:T(8,128)S(1)}, u32[]{:S(2)}, u32[]{:S(2)}) collective-permute-start(f32[512,768]{1,0:T(8,128)S(1)} %convolution_add_fusion), channel_id=1, source_target_pairs={{1,0},{2,1},{3,2},{4,3},{5,4},{6,5},{7,6},{8,7},{9,8},{10,9},{11,1... | collective-permute-start | bytes 4718600 | tf_op jit(solution)/shard_map/ppermute | solution.py:10
where the time goes:
time: 91.7 us; the launch traced here: 91.4 us
  waiting for transfers between devices  64.9 us (71%)
  starting transfers between devices  13.9 us (15%)
  matrix products  8.68 us (9%)
  between operations  2.02 us (2%)
  other arithmetic  1.91 us (2%)
    ppermute x4, waiting for transfers between devices, from_behind(): return lax.ppermute(block, axis, route)  64.9 us
    ppermute x4, starting transfers between devices, from_behind(): return lax.ppermute(block, axis, route)  13.9 us
    dot_general x3, matrix products, score_block(): inner = jnp.dot(images, texts.T, preferred_element_type=jnp.float32)  3.46 us
    dot_general x3, matrix products, score_block(): grad_rows = jnp.dot(coeff, texts, preferred_element_type=jnp.float32)  3.1 us
    dot_general x3, matrix products, score_block(): partial_cols = jnp.dot(coeff.T, images, preferred_element_type=jnp.float32)  2.11 us
  transfers between devices with their start and end apart: 4, of which 4 were waited for; matrix products, arithmetic and copies ran while one was open for 7% of the time, Pallas kernels for 0%

commit v1 on v0

v1 whole, which is shorter than its diff:
```python
import functools

import jax
import jax.numpy as jnp
from jax import lax
from jax.experimental import pallas as pl
from jax.experimental.pallas import tpu as pltpu
from jax.sharding import PartitionSpec as P

MESH = pl.DeviceIdType.MESH
PARTS = 4
WIDE = 256
NT = (((1,), (1,)), ((), ()))


def work(own, other, acc, loss, scale, bias, diagonal=None):
    columns = other.shape[0]
    logits = scale * lax.dot_general(own, other, NT, preferred_element_type=jnp.float32) + bias
    small = jnp.exp(-jnp.abs(logits))
    inverse = 1.0 / (1.0 + small)
    sigmoid = jnp.where(logits >= 0.0, inverse, small * inverse)
    signed = logits
    if diagonal is not None:
        rows = lax.broadcasted_iota(jnp.int32, logits.shape, 0)
        match = lax.broadcasted_iota(jnp.int32, logits.shape, 1) + diagonal == rows
        sigmoid = sigmoid - jnp.where(match, 1.0, 0.0)
        signed = jnp.where(match, -logits, logits)
    losses = jnp.maximum(signed, 0.0) + jnp.log1p(small)
    coeff = (scale * sigmoid).astype(jnp.bfloat16)
    acc[...] += jnp.dot(coeff, other, preferred_element_type=jnp.float32)
    total = losses[:, 0:128]
    for first in range(128, columns, 128):
        total += losses[:, first:first + 128]
    loss[...] += total


def kernel(devices, image_ref, text_ref, scale_ref, bias_ref, loss_ref, gimage_ref, gtext_ref,
           x, y, z1, z2, w1, w2, accx, accy, lossx, lossy, load_sem, out_sem, send, recv):
    me = lax.axis_index("dp")
    core = lax.rem(me, 2)
    step = 2 * core - 1
    partner = me - step
    near = lax.rem(me + step + devices, devices)
    far = lax.rem(me + 2 * step + devices, devices)
    behind = lax.rem(me - 2 * step + devices, devices)
    rows = x.shape[0]
    part = rows // PARTS

    barrier = pltpu.get_barrier_semaphore()
    for other in (partner, near, far, behind):
        pl.semaphore_signal(barrier, inc=1, device_id=(other,), device_id_type=MESH)

    def load(source, target, slot):
        return pltpu.make_async_copy(source, target, load_sem.at[slot])

    @pl.when(core == 1)
    def _():
        load(text_ref, x, 0).start()
        load(image_ref, y, 1).start()

    @pl.when(core == 0)
    def _():
        load(image_ref, x, 0).start()
        load(text_ref, y, 1).start()

    accx[...] = jnp.zeros_like(accx)
    accy[...] = jnp.zeros_like(accy)
    lossx[...] = jnp.zeros_like(lossx)
    lossy[...] = jnp.zeros_like(lossy)
    scale = scale_ref[0]
    bias = bias_ref[0]
    load(image_ref, x, 0).wait()
    load(text_ref, y, 1).wait()

    def remote(source, target, way, index, device):
        piece = pl.ds(pl.multiple_of(index * part, part), part)
        return pltpu.make_async_remote_copy(
            src_ref=source.at[piece], dst_ref=target.at[piece], send_sem=send.at[way, index],
            recv_sem=recv.at[way, index], device_id=(device,), device_id_type=MESH)

    def to_partner(index):
        return remote(y, z1, 0, index, partner)

    def to_far(index):
        return remote(x, z2, 1, index, far)

    def to_near(index):
        return remote(z1, w2, 2, index, near)

    def relay(index):
        return remote(z2, w1, 3, index, partner)

    def each(action):
        def run(index, carry):
            action(index)
            return carry
        lax.fori_loop(0, PARTS, run, 0)

    pl.semaphore_wait(barrier, 4)
    each(lambda index: to_far(index).start())
    each(lambda index: to_partner(index).start())

    def wide(action):
        def run(index, carry):
            start = pl.multiple_of(index * WIDE, WIDE)
            action(start, pl.ds(start, WIDE))
            return carry
        lax.fori_loop(0, rows // WIDE, run, 0)

    wide(lambda start, piece: work(y[...], x[piece, :], accy, lossy, scale, bias, start))
    wide(lambda start, piece: work(x[...], y[piece, :], accx, lossx, scale, bias, start))

    def forward(index):
        to_partner(index).wait_recv()
        to_near(index).start()

    each(forward)
    wide(lambda start, piece: work(y[...], z1[piece, :], accy, lossy, scale, bias))

    def visiting(index):
        piece = pl.ds(pl.multiple_of(index * part, part), part)
        to_far(index).wait_recv()
        relay(index).start()
        work(y[...], z2[piece, :], accy, lossy, scale, bias)
        relay(index).wait_recv()
        work(x[...], w1[piece, :], accx, lossx, scale, bias)

    each(visiting)

    def store(source, target, slot):
        return pltpu.make_async_copy(source, target, out_sem.at[slot])

    @pl.when(core == 1)
    def _():
        store(accy, gimage_ref, 0).start()

    @pl.when(core == 0)
    def _():
        store(accy, gtext_ref, 0).start()

    def last(index):
        piece = pl.ds(pl.multiple_of(index * part, part), part)
        to_near(index).wait_recv()
        work(x[...], w2[piece, :], accx, lossx, scale, bias)

    each(last)

    @pl.when(core == 1)
    def _():
        store(accx, gtext_ref, 1).start()

    @pl.when(core == 0)
    def _():
        store(accx, gimage_ref, 1).start()

    lanes = jnp.where(core == 1, lossy[...], lossx[...])
    loss_ref[...] = jnp.sum(lanes.T, axis=0, keepdims=True) / (3.0 * rows)

    def drain(index):
        to_partner(index).wait_send()
        to_far(index).wait_send()
        to_near(index).wait_send()
        relay(index).wait_send()

    each(drain)
    store(accy, gimage_ref, 0).wait()
    store(accx, gtext_ref, 1).wait()


def body(image_embed, text_embed, logit_scale, logit_bias):
    rows, width = image_embed.shape
    devices = lax.axis_size("dp")
    block = pltpu.VMEM((rows, width), jnp.bfloat16)
    wide = pltpu.VMEM((rows, width), jnp.float32)
    lanes = pltpu.VMEM((rows, 128), jnp.float32)
    hbm = pl.BlockSpec(memory_space=pl.ANY)
    smem = pl.BlockSpec(memory_space=pltpu.SMEM)
    loss, grad_image, grad_text = pl.pallas_call(
        functools.partial(kernel, devices),
        out_shape=(
            jax.ShapeDtypeStruct((1, rows), jnp.float32),
            jax.ShapeDtypeStruct((rows, width), jnp.float32),
            jax.ShapeDtypeStruct((rows, width), jnp.float32),
        ),
        in_specs=[hbm, hbm, smem, smem],
        out_specs=(pl.BlockSpec(memory_space=pltpu.VMEM), hbm, hbm),
        scratch_shapes=[
            block, block, block, block, block, block, wide, wide, lanes, lanes,
            pltpu.SemaphoreType.DMA((2,)), pltpu.SemaphoreType.DMA((2,)),
            pltpu.SemaphoreType.DMA((4, PARTS)), pltpu.SemaphoreType.DMA((4, PARTS)),
        ],
        compiler_params=pltpu.CompilerParams(
            collective_id=0, has_side_effects=True, vmem_limit_bytes=48 << 20),
        name="sigmoid_ring",
    )(image_embed, text_embed, logit_scale, logit_bias)
    return loss.reshape(rows), grad_image, grad_text


def solution(mesh):
    in_specs = (P("dp", None), P("dp", None), P(), P())
    out_specs = (P("dp"), P("dp", None), P("dp", None))
    return jax.shard_map(body, mesh=mesh, in_specs=in_specs, out_specs=out_specs, check_vma=False)
```

time: 91.7 us -> 45 us (0.49)
  the two profiles are of different devices: /device:TPU:6 before, /device:TPU:1 now
where the time goes in v1:
time: 45 us; the launch traced here: 44.8 us
  Pallas kernels  37.7 us (84%)
  local copies, waits for them, and re-layouts  5.12 us (11%)
  between operations  1.94 us (4%)
    pallas_call x1, Pallas kernels, body(): pl.pallas_call(functools.partial(kernel, devices), out_shape=(jax.ShapeDt...  37.7 us
    unnamed x7, local copies, waits for them, and re-layouts  5.12 us

profile of v1, /device:TPU:1, one launch (start us, length us, event | category | flops | bytes accessed | tf_op | source)
XLA Modules:
  0.0 44.8 jit_solution(5218912966779440791)
XLA Ops:
  1.9 0.0 copy-start
  1.9 1.1 %copy-done = bf16[512,768]{1,0:T(8,128)(2,1)S(1)} copy-done((bf16[512,768]{1,0:T(8,128)(2,1)S(1)}, bf16[512,768]{1,0:T(8,128)(2,1)}, u32[]{:S(2)}) %copy-start) | copy-done | bytes 786456
  3.1 0.0 copy-start.1
  3.1 1.1 %copy-done.1 = bf16[512,768]{1,0:T(8,128)(2,1)S(1)} copy-done((bf16[512,768]{1,0:T(8,128)(2,1)S(1)}, bf16[512,768]{1,0:T(8,128)(2,1)}, u32[]{:S(2)}) %copy-start.1) | copy-done | bytes 786456
  4.2 37.7 %sigmoid_ring.1 = (f32[1,512]{1,0:T(1,128)S(1)}, f32[512,768]{1,0:T(8,128)S(1)}, f32[512,768]{1,0:T(8,128)S(1)}) custom-call(bf16[512,768]{1,0:T(8,128)(2,1)S(1)} %copy-done, bf16[512,768]{1,0:T(8,128)(2,1)S(1)} %copy-done.1, f32[1]{0:T(128)S(6)} %copy.10.scale_ref, f32[1]{0:T(128)S(6)} %copy.11.bias_ref), custom_call_target="tpu_custom_call" | custom-call | tf_op jit(solution)/shard_map/sigmoid_ring/pallas_call | solution.py:178
  41.9 0.6 %copy.12 = f32[512]{0:T(512)} copy(f32[512]{0:T(512)S(1)} %bitcast.1) | data formatting | bytes 4096
  42.5 1.1 %copy.13 = f32[512,768]{1,0:T(8,128)} copy(f32[512,768]{1,0:T(8,128)S(1)} %get-tuple-element.13) | data formatting | bytes 3145728
  43.6 1.1 %copy.14 = f32[512,768]{1,0:T(8,128)} copy(f32[512,768]{1,0:T(8,128)S(1)} %get-tuple-element.14) | data formatting | bytes 3145728
Async XLA Ops:
  1.9 1.1 %copy-start = (bf16[512,768]{1,0:T(8,128)(2,1)S(1)}, bf16[512,768]{1,0:T(8,128)(2,1)}, u32[]{:S(2)}) copy-start(bf16[512,768]{1,0:T(8,128)(2,1)} %image_ref.1) | copy-start | bytes 2359300
  3.1 1.1 %copy-start.1 = (bf16[512,768]{1,0:T(8,128)(2,1)S(1)}, bf16[512,768]{1,0:T(8,128)(2,1)}, u32[]{:S(2)}) copy-start(bf16[512,768]{1,0:T(8,128)(2,1)} %text_ref.1) | copy-start | bytes 2359300

commit v2 on v1

v2 whole, which is shorter than its diff:
```python
import functools

import jax
import jax.numpy as jnp
from jax import lax
from jax.experimental import pallas as pl
from jax.experimental.pallas import tpu as pltpu
from jax.sharding import PartitionSpec as P

MESH = pl.DeviceIdType.MESH
PARTS = 4
WIDE = 256
GATE = 2
NT = (((1,), (1,)), ((), ()))
PARTNER, DIRECT, RELAYED, SECOND = 0, 1, 2, 3


def work(own, other, acc, loss, scale, bias, diagonal=None):
    columns = other.shape[0]
    logits = scale * lax.dot_general(own, other, NT, preferred_element_type=jnp.float32) + bias
    small = jnp.exp(-jnp.abs(logits))
    inverse = 1.0 / (1.0 + small)
    sigmoid = jnp.where(logits >= 0.0, inverse, small * inverse)
    signed = logits
    if diagonal is not None:
        rows = lax.broadcasted_iota(jnp.int32, logits.shape, 0)
        match = lax.broadcasted_iota(jnp.int32, logits.shape, 1) + diagonal == rows
        sigmoid = sigmoid - jnp.where(match, 1.0, 0.0)
        signed = jnp.where(match, -logits, logits)
    losses = jnp.maximum(signed, 0.0) + jnp.log1p(small)
    coeff = (scale * sigmoid).astype(jnp.bfloat16)
    acc[...] += jnp.dot(coeff, other, preferred_element_type=jnp.float32)
    total = losses[:, 0:128]
    for first in range(128, columns, 128):
        total += losses[:, first:first + 128]
    loss[...] += total


def ring_kernel(devices, image_ref, text_ref, scale_ref, bias_ref, acc, loss,
                own, blocks, load_sem, send, recv, ready):
    me = lax.axis_index("dp")
    core = lax.rem(me, 2)
    step = 2 * core - 1
    partner = me - step
    near = lax.rem(me + step + devices, devices)
    far = lax.rem(me + 2 * step + devices, devices)
    rows = own.shape[1]
    part = rows // PARTS

    barrier = pltpu.get_barrier_semaphore()
    previous = lax.rem(me - 1 - core + devices, devices)
    for other in (partner, previous):
        pl.semaphore_signal(barrier, inc=1, device_id=(other,), device_id_type=MESH)

    def load(source, target, slot):
        return pltpu.make_async_copy(source, target, load_sem.at[slot])

    load(image_ref, own.at[0], 0).start()
    load(text_ref, own.at[1], 1).start()
    acc[...] = jnp.zeros_like(acc)
    loss[...] = jnp.zeros_like(loss)
    scale = scale_ref[0]
    bias = bias_ref[0]
    load(image_ref, own.at[0], 0).wait()
    load(text_ref, own.at[1], 1).wait()

    def piece_of(index):
        return pl.ds(pl.multiple_of(index * part, part), part)

    def remote(source, way, index, device):
        return pltpu.make_async_remote_copy(
            src_ref=source.at[piece_of(index)], dst_ref=blocks.at[way, piece_of(index)],
            send_sem=send.at[way, index], recv_sem=recv.at[way, index],
            device_id=(device,), device_id_type=MESH)

    def to_partner(index):
        return remote(own.at[1 - core], PARTNER, index, partner)

    def to_far(index):
        return remote(own.at[core], DIRECT, index, far)

    def relay(index):
        return remote(blocks.at[DIRECT], RELAYED, index, partner)

    def to_near(index):
        return remote(blocks.at[PARTNER], SECOND, index, near)

    def each(action, first=0, last=PARTS):
        def run(index, carry):
            action(index)
            return carry
        lax.fori_loop(first, last, run, 0)

    @pl.when(core == 1)
    def _():
        pl.semaphore_wait(barrier, 3)
        pl.semaphore_signal(ready, inc=1, device_id=(near,), device_id_type=MESH)

    @pl.when(core == 0)
    def _():
        pl.semaphore_wait(barrier, 1)

    each(lambda index: to_partner(index).start())

    @pl.when(core == 0)
    def _():
        pl.semaphore_wait(ready, 1)

    each(lambda index: to_far(index).start())

    def wide(action):
        def run(index, carry):
            start = pl.multiple_of(index * WIDE, WIDE)
            action(start, pl.ds(start, WIDE))
            return carry
        lax.fori_loop(0, rows // WIDE, run, 0)

    wide(lambda start, piece: work(own[0], own[1, piece], acc.at[0], loss.at[0], scale, bias, start))
    wide(lambda start, piece: work(own[1], own[0, piece], acc.at[1], loss.at[1], scale, bias, start))

    each(lambda index: to_far(index).wait_send(), 0, GATE)

    def forward(index):
        to_partner(index).wait_recv()
        to_near(index).start()

    each(forward)
    wide(lambda start, piece: work(
        own[1 - core], blocks[PARTNER, piece], acc.at[1 - core], loss.at[1 - core], scale, bias))

    def visit(index, carry):
        phase = lax.div(index, PARTS)
        chunk = lax.rem(index, PARTS)
        slot = 1 + phase
        side = jnp.where(slot == DIRECT, 1 - core, core)
        piece = piece_of(chunk)
        pltpu.make_async_remote_copy(
            src_ref=blocks.at[slot, piece], dst_ref=blocks.at[slot, piece],
            send_sem=send.at[slot, chunk], recv_sem=recv.at[slot, chunk],
            device_id=(partner,), device_id_type=MESH).wait_recv()

        @pl.when(slot == DIRECT)
        def _():
            relay(chunk).start()

        work(own[side], blocks[slot, piece], acc.at[side], loss.at[side], scale, bias)
        return carry

    lax.fori_loop(0, 3 * PARTS, visit, 0)

    each(lambda index: to_far(index).wait_send(), GATE)

    def drain(index):
        to_partner(index).wait_send()
        to_near(index).wait_send()
        relay(index).wait_send()

    each(drain)


def finish_kernel(acc, loss, loss_ref, image_ref, text_ref, sems):
    rows = loss.shape[1]
    stores = [
        pltpu.make_async_copy(acc.at[side], target, sems.at[side])
        for side, target in ((0, image_ref), (1, text_ref))
    ]
    for store in stores:
        store.start()
    loss_ref[...] = jnp.sum(loss[0].T, axis=0, keepdims=True) / (3.0 * rows)
    for store in stores:
        store.wait()


def body(image_embed, text_embed, logit_scale, logit_bias):
    rows, width = image_embed.shape
    devices = lax.axis_size("dp")
    anywhere = pl.BlockSpec(memory_space=pl.ANY)
    smem = pl.BlockSpec(memory_space=pltpu.SMEM)
    hbm = pl.BlockSpec(memory_space=pltpu.HBM)
    vmem = pl.BlockSpec(memory_space=pltpu.VMEM)
    image_embed, text_embed = (pltpu.with_memory_space_constraint(a, pltpu.HBM) for a in (image_embed, text_embed))
    acc, loss = pl.pallas_call(
        functools.partial(ring_kernel, devices),
        out_shape=(
            pltpu.VMEM((2, rows, width), jnp.float32),
            pltpu.VMEM((2, rows, 128), jnp.float32),
        ),
        in_specs=[hbm, hbm, smem, smem],
        out_specs=(vmem, vmem),
        scratch_shapes=[
            pltpu.VMEM((2, rows, width), jnp.bfloat16),
            pltpu.VMEM((4, rows, width), jnp.bfloat16),
            pltpu.SemaphoreType.DMA((2,)),
            pltpu.SemaphoreType.DMA((4, PARTS)),
            pltpu.SemaphoreType.DMA((4, PARTS)),
            pltpu.SemaphoreType.REGULAR,
        ],
        compiler_params=pltpu.CompilerParams(
            collective_id=0, has_side_effects=True, vmem_limit_bytes=32 << 20),
        name="sigmoid_ring",
    )(image_embed, text_embed, logit_scale, logit_bias)
    acc, loss = (pltpu.with_memory_space_constraint(a, pltpu.VMEM) for a in (acc, loss))
    row_loss, grad_image, grad_text = pl.pallas_call(
        finish_kernel,
        out_shape=(
            jax.ShapeDtypeStruct((1, rows), jnp.float32),
            jax.ShapeDtypeStruct((rows, width), jnp.float32),
            jax.ShapeDtypeStruct((rows, width), jnp.float32),
        ),
        in_specs=[vmem, vmem],
        out_specs=(vmem, anywhere, anywhere),
        scratch_shapes=[pltpu.SemaphoreType.DMA((2,))],
        compiler_params=pltpu.CompilerParams(vmem_limit_bytes=4 << 20),
        name="finish",
    )(acc, loss)
    return row_loss.reshape(rows), grad_image, grad_text


def solution(mesh):
    in_specs = (P("dp", None), P("dp", None), P(), P())
    out_specs = (P("dp"), P("dp", None), P("dp", None))
    return jax.shard_map(body, mesh=mesh, in_specs=in_specs, out_specs=out_specs, check_vma=False)
```

time: 45 us -> 40.3 us (0.90)
  local copies, waits for them, and re-layouts: 5.12 us -> 0 us
  Pallas kernels: 37.7 us -> 38.2 us
    unnamed x7 -> x0, local copies, waits for them, and re-layouts: 5.12 us -> none
    pallas_call x1 -> x2, Pallas kernels: 37.7 us -> 38.2 us  [the longest x1 35.9 us: body(): pl.pallas_call(functools.partial(ring_kernel, devices), out_shape=(pltpu....]
where the time goes in v2:
time: 40.3 us; the launch traced here: 40.1 us
  Pallas kernels  38.2 us (95%)
  between operations  1.93 us (5%)
    pallas_call x1, Pallas kernels, body(): pl.pallas_call(functools.partial(ring_kernel, devices), out_shape=(pltpu....  35.9 us
    pallas_call x1, Pallas kernels, body(): pl.pallas_call(finish_kernel, out_shape=(jax.ShapeDtypeStruct((1, rows),...  2.27 us

profile of v2, /device:TPU:1, one launch (start us, length us, event | category | flops | bytes accessed | tf_op | source)
XLA Modules:
  0.0 40.1 jit_solution(10429622667917210015)
XLA Ops:
  1.9 35.9 %sigmoid_ring.1 = (f32[2,512,768]{2,1,0:T(8,128)S(1)}, f32[2,512,128]{2,1,0:T(8,128)S(1)}) custom-call(bf16[512,768]{1,0:T(8,128)(2,1)} %image_ref.1, bf16[512,768]{1,0:T(8,128)(2,1)} %text_ref.1, f32[1]{0:T(128)S(6)} %copy.7.scale_ref, f32[1]{0:T(128)S(6)} %copy.8.bias_ref), custom_call_target="tpu_custom_call" | custom-call | tf_op jit(solution)/shard_map/sigmoid_ring/pallas_call | solution.py:182
  37.8 2.3 %finish.1 = (f32[1,512]{1,0:T(1,128)}, f32[512,768]{1,0:T(8,128)}, f32[512,768]{1,0:T(8,128)}) custom-call(f32[2,512,768]{2,1,0:T(8,128)S(1)} %get-tuple-element.8.acc, f32[2,512,128]{2,1,0:T(8,128)S(1)} %get-tuple-element.9.loss), custom_call_target="tpu_custom_call" | custom-call | tf_op jit(solution)/shard_map/finish/pallas_call | solution.py:203

commit v3 on v2

v3 whole, which is shorter than its diff:
```python
import functools

import jax
import jax.numpy as jnp
from jax import lax
from jax.experimental import pallas as pl
from jax.experimental.pallas import tpu as pltpu
from jax.sharding import PartitionSpec as P

MESH = pl.DeviceIdType.MESH
PARTS = 4
TILES = 4
NT = (((1,), (1,)), ((), ()))
PARTNER, DIRECT, RELAYED, SECOND = 0, 1, 2, 3


def score(own, other, scale, bias, diagonal=False):
    logits = scale * lax.dot_general(own, other, NT, preferred_element_type=jnp.float32) + bias
    small = jnp.exp(-jnp.abs(logits))
    inverse = 1.0 / (1.0 + small)
    sigmoid = jnp.where(logits >= 0.0, inverse, small * inverse)
    signed = logits
    if diagonal:
        rows = lax.broadcasted_iota(jnp.int32, logits.shape, 0)
        match = lax.broadcasted_iota(jnp.int32, logits.shape, 1) == rows
        sigmoid = sigmoid - jnp.where(match, 1.0, 0.0)
        signed = jnp.where(match, -logits, logits)
    losses = jnp.maximum(signed, 0.0) + jnp.log1p(small)
    total = losses[:, 0:128]
    for first in range(128, losses.shape[1], 128):
        total += losses[:, first:first + 128]
    return total, (scale * sigmoid).astype(jnp.bfloat16)


def work(own, other, acc, loss, scale, bias):
    losses, coeff = score(own, other, scale, bias)
    acc[...] += jnp.dot(coeff, other, preferred_element_type=jnp.float32)
    loss[...] += losses


def ring_kernel(devices, image_ref, text_ref, scale_ref, bias_ref, acc, loss, own, second,
                blocks, load_sem, send, recv, here, ready):
    me = lax.axis_index("dp")
    core = lax.rem(me, 2)
    step = 2 * core - 1
    partner = me - step
    near = lax.rem(me + step + devices, devices)
    far = lax.rem(me + 2 * step + devices, devices)
    rows = own.shape[1]
    part = rows // PARTS

    barrier = pltpu.get_barrier_semaphore()
    previous = lax.rem(me - 1 - core + devices, devices)
    pl.semaphore_signal(barrier, inc=1, device_id=(previous,), device_id_type=MESH)

    @pl.when(core == 1)
    def _():
        pl.semaphore_signal(barrier, inc=1, device_id=(partner,), device_id_type=MESH)

    loads = [
        pltpu.make_async_copy(source, target, load_sem.at[slot])
        for slot, (source, target) in enumerate(((image_ref, own.at[0]), (text_ref, own.at[1])))
    ]

    def piece_of(index):
        return pl.ds(pl.multiple_of(index * part, part), part)

    def remote(source, way, index, device):
        target = second if way == SECOND else blocks.at[way]
        return pltpu.make_async_remote_copy(
            src_ref=source.at[piece_of(index)], dst_ref=target.at[piece_of(index)],
            send_sem=send.at[way, index], recv_sem=recv.at[way, index],
            device_id=(device,), device_id_type=MESH)

    def to_partner(source, index):
        return remote(source, PARTNER, index, partner)

    def to_far(source, index):
        return remote(source, DIRECT, index, far)

    def relay(index):
        return remote(blocks.at[DIRECT], RELAYED, index, partner)

    def to_near(index):
        return remote(blocks.at[PARTNER], SECOND, index, near)

    def each(action, first=0, last=PARTS):
        def run(index, carry):
            action(index)
            return carry
        lax.fori_loop(first, last, run, 0)

    @pl.when(core == 1)
    def _():
        pl.semaphore_wait(barrier, 2)
        each(lambda index: to_far(text_ref, index).start())
        pl.semaphore_wait(here, 1)
        pl.semaphore_signal(ready, inc=1, device_id=(near,), device_id_type=MESH)
        each(lambda index: to_partner(image_ref, index).start())
        for load in loads:
            load.start()

    @pl.when(core == 0)
    def _():
        pl.semaphore_wait(barrier, 1)
        pl.semaphore_signal(here, inc=1, device_id=(partner,), device_id_type=MESH)
        each(lambda index: to_partner(text_ref, index).start())
        for load in loads:
            load.start()
        pl.semaphore_wait(ready, 1)
        each(lambda index: to_far(image_ref, index).start())

    for load in loads:
        load.wait()
    scale = scale_ref[0]
    bias = bias_ref[0]

    for side in (0, 1):
        losses, coeff = score(own[side], own[1 - side], scale, bias, diagonal=True)
        acc[side] = jnp.dot(coeff, own[1 - side], preferred_element_type=jnp.float32)
        loss[side] = losses

    def visit(slot, carry):
        @pl.when(slot == PARTNER)
        def _():
            each(lambda index: to_partner(own.at[1 - core], index).wait_recv())

        @pl.when(slot == DIRECT)
        def _():
            each(lambda index: to_far(own.at[core], index).wait_send(), 0, PARTS - 1)
            to_near(0).start()
            to_far(own.at[core], PARTS - 1).wait_send()
            each(lambda index: to_near(index).start(), 1)

            def pass_on(index):
                to_far(own.at[core], index).wait_recv()
                relay(index).start()

            each(pass_on)

        @pl.when(slot == RELAYED)
        def _():
            each(lambda index: relay(index).wait_recv())

        side = jnp.where(slot == RELAYED, core, 1 - core)
        work(own[side], blocks[slot], acc.at[side], loss.at[side], scale, bias)
        return carry

    lax.fori_loop(PARTNER, SECOND, visit, 0)

    to_near(0).wait_recv()
    to_near(1).wait_recv()
    half = rows // 2
    work(own[core], second[0:half], acc.at[core], loss.at[core], scale, bias)
    to_near(2).wait_recv()
    work(own[core], second[half:half + part], acc.at[core], loss.at[core], scale, bias)

    def drain(index):
        to_partner(own.at[1 - core], index).wait_send()
        to_near(index).wait_send()
        relay(index).wait_send()

    each(drain)
    to_near(3).wait_recv()


def finish_kernel(acc, loss, own, second, scale_ref, bias_ref, loss_ref, image_ref, text_ref, row_loss, sems):
    core = lax.rem(lax.axis_index("dp"), 2)
    rows = loss.shape[1]
    tile = rows // TILES
    scale = scale_ref[0]
    bias = bias_ref[0]
    last = second[rows - rows // PARTS:]

    def store(side, target, slot, piece):
        return pltpu.make_async_copy(acc.at[side, piece], target.at[piece], sems.at[slot])

    whole = pl.ds(0, rows)

    def both(action):
        @pl.when(core == 1)
        def _():
            action(image_ref, text_ref)

        @pl.when(core == 0)
        def _():
            action(text_ref, image_ref)

    both(lambda done, open_: store(1 - core, done, TILES, whole).start())
    for index in range(TILES):
        piece = pl.ds(index * tile, tile)
        losses, coeff = score(own[core, piece], last, scale, bias)
        acc[core, piece] += jnp.dot(coeff, last, preferred_element_type=jnp.float32)
        loss[core, piece] += losses
        both(lambda done, open_: store(core, open_, index, piece).start())

    row_loss[...] = jnp.sum(loss[0].T, axis=0, keepdims=True) / (3.0 * rows)
    row_copy = pltpu.make_async_copy(row_loss, loss_ref, sems.at[TILES + 1])
    row_copy.start()
    store(1 - core, image_ref, TILES, whole).wait()
    for index in range(TILES):
        store(core, image_ref, index, pl.ds(index * tile, tile)).wait()
    row_copy.wait()


def body(image_embed, text_embed, logit_scale, logit_bias):
    rows, width = image_embed.shape
    devices = lax.axis_size("dp")
    anywhere = pl.BlockSpec(memory_space=pl.ANY)
    smem = pl.BlockSpec(memory_space=pltpu.SMEM)
    hbm = pl.BlockSpec(memory_space=pltpu.HBM)
    vmem = pl.BlockSpec(memory_space=pltpu.VMEM)
    images, texts = (pltpu.with_memory_space_constraint(a, pltpu.HBM) for a in (image_embed, text_embed))
    state = pl.pallas_call(
        functools.partial(ring_kernel, devices),
        out_shape=(
            pltpu.VMEM((2, rows, width), jnp.float32),
            pltpu.VMEM((2, rows, 128), jnp.float32),
            pltpu.VMEM((2, rows, width), jnp.bfloat16),
            pltpu.VMEM((rows, width), jnp.bfloat16),
        ),
        in_specs=[hbm, hbm, smem, smem],
        out_specs=(vmem, vmem, vmem, vmem),
        scratch_shapes=[
            pltpu.VMEM((3, rows, width), jnp.bfloat16),
            pltpu.SemaphoreType.DMA((2,)),
            pltpu.SemaphoreType.DMA((4, PARTS)),
            pltpu.SemaphoreType.DMA((4, PARTS)),
            pltpu.SemaphoreType.REGULAR,
            pltpu.SemaphoreType.REGULAR,
        ],
        compiler_params=pltpu.CompilerParams(
            collective_id=0, has_side_effects=True, vmem_limit_bytes=32 << 20),
        name="sigmoid_ring",
    )(images, texts, logit_scale, logit_bias)
    state = [pltpu.with_memory_space_constraint(a, pltpu.VMEM) for a in state]
    row_loss, grad_image, grad_text = pl.pallas_call(
        finish_kernel,
        out_shape=(
            jax.ShapeDtypeStruct((1, rows), jnp.float32),
            jax.ShapeDtypeStruct((rows, width), jnp.float32),
            jax.ShapeDtypeStruct((rows, width), jnp.float32),
        ),
        in_specs=[vmem, vmem, vmem, vmem, smem, smem],
        out_specs=(anywhere, anywhere, anywhere),
        scratch_shapes=[pltpu.VMEM((1, rows), jnp.float32), pltpu.SemaphoreType.DMA((TILES + 2,))],
        compiler_params=pltpu.CompilerParams(vmem_limit_bytes=8 << 20),
        name="finish",
    )(*state, logit_scale, logit_bias)
    return row_loss.reshape(rows), grad_image, grad_text


def solution(mesh):
    in_specs = (P("dp", None), P("dp", None), P(), P())
    out_specs = (P("dp"), P("dp", None), P("dp", None))
    return jax.shard_map(body, mesh=mesh, in_specs=in_specs, out_specs=out_specs, check_vma=False)
```

time: 40.3 us -> 36.1 us (0.90)
  Pallas kernels: 38.2 us -> 34 us
    pallas_call x1, Pallas kernels: 35.9 us -> 32.2 us  [body(): pl.pallas_call(functools.partial(ring_kernel, devices), out_shape=(pltpu....]
    pallas_call x1, Pallas kernels: 2.27 us -> 1.85 us  [body(): pl.pallas_call(finish_kernel, out_shape=(jax.ShapeDtypeStruct((1, rows),...]
where the time goes in v3:
time: 36.1 us; the launch traced here: 36 us
  Pallas kernels  34 us (94%)
  between operations  1.93 us (5%)
    pallas_call x1, Pallas kernels, body(): pl.pallas_call(functools.partial(ring_kernel, devices), out_shape=(pltpu....  32.2 us
    pallas_call x1, Pallas kernels, body(): pl.pallas_call(finish_kernel, out_shape=(jax.ShapeDtypeStruct((1, rows),...  1.85 us

profile of v3, /device:TPU:1, one launch (start us, length us, event | category | flops | bytes accessed | tf_op | source)
XLA Modules:
  0.0 36.0 jit_solution(2602185019495060564)
XLA Ops:
  1.9 32.2 %sigmoid_ring.1 = (f32[2,512,768]{2,1,0:T(8,128)S(1)}, f32[2,512,128]{2,1,0:T(8,128)S(1)}, bf16[2,512,768]{2,1,0:T(8,128)(2,1)S(1)}, bf16[512,768]{1,0:T(8,128)(2,1)S(1)}) custom-call(bf16[512,768]{1,0:T(8,128)(2,1)} %image_ref.1, bf16[512,768]{1,0:T(8,128)(2,1)} %text_ref.1, f32[1]{0:T(128)S(6)} %copy.7.scale_ref, f32[1]{0:T(128)S(6)} %copy.8.bias_ref), custom_call_target="tpu_custom_call" | custom-call | tf_op jit(solution)/shard_map/sigmoid_ring/pallas_call | solution.py:214
  34.1 1.9 %finish.1 = (f32[1,512]{1,0:T(1,128)}, f32[512,768]{1,0:T(8,128)}, f32[512,768]{1,0:T(8,128)}) custom-call(f32[2,512,768]{2,1,0:T(8,128)S(1)} %get-tuple-element.10.acc, f32[2,512,128]{2,1,0:T(8,128)S(1)} %get-tuple-element.11.loss, bf16[2,512,768]{2,1,0:T(8,128)(2,1)S(1)} %get-tuple-element.12.own, bf16[512,768]{1,0:T(8,128)(2,1)S(1)} %get-tuple-element.13.second, ...), custom_call_target="tpu_custom_call" | custom-call | tf_op jit(solution)/shard_map/finish/pallas_call | solution.py:237

commit v4 on v3

--- a/solution.py
+++ b/solution.py
@@ -10,6 +10,7 @@
 MESH = pl.DeviceIdType.MESH
 PARTS = 4
 TILES = 4
+HEIGHT, DEPTH = 4, 16
 NT = (((1,), (1,)), ((), ()))
 PARTNER, DIRECT, RELAYED, SECOND = 0, 1, 2, 3
 
@@ -120,40 +121,61 @@
         acc[side] = jnp.dot(coeff, own[1 - side], preferred_element_type=jnp.float32)
         loss[side] = losses
 
-    def visit(slot, carry):
+    def follow():
+        each(lambda index: to_far(own.at[core], index).wait_send(), 0, PARTS - 1)
+        to_near(0).start()
+        to_far(own.at[core], PARTS - 1).wait_send()
+        each(lambda index: to_near(index).start(), 1)
+
+    def pass_on():
+        def run(index):
+            to_far(own.at[core], index).wait_recv()
+            relay(index).start()
+        each(run)
+
+    chip = lax.div(me, 2)
+    starts = lax.rem(chip, DEPTH) == 0
+    corner = lax.rem(lax.div(chip, DEPTH), HEIGHT) == 0
+    early_images = jnp.logical_and(starts, core == 0)
+    late_texts = jnp.logical_and(starts, core == 1)
+
+    def visit(phase, carry):
+        slot = jnp.where(late_texts, jnp.where(phase == PARTNER, PARTNER, jnp.where(
+            phase == 1, RELAYED, jnp.where((phase == 2) == corner, SECOND, DIRECT))), phase)
+
         @pl.when(slot == PARTNER)
         def _():
             each(lambda index: to_partner(own.at[1 - core], index).wait_recv())
 
-        @pl.when(slot == DIRECT)
-        def _():
-            each(lambda index: to_far(own.at[core], index).wait_send(), 0, PARTS - 1)
-            to_near(0).start()
-            to_far(own.at[core], PARTS - 1).wait_send()
-            each(lambda index: to_near(index).start(), 1)
-
-            def pass_on(index):
-                to_far(own.at[core], index).wait_recv()
-                relay(index).start()
-
-            each(pass_on)
+        @pl.when(jnp.logical_and(slot == DIRECT, jnp.logical_not(early_images)))
+        def _():
+            pass_on()
 
         @pl.when(slot == RELAYED)
         def _():
             each(lambda index: relay(index).wait_recv())
 
-        side = jnp.where(slot == RELAYED, core, 1 - core)
-        work(own[side], blocks[slot], acc.at[side], loss.at[side], scale, bias)
+        @pl.when(slot != SECOND)
+        def _():
+            side = jnp.where(slot == RELAYED, core, 1 - core)
+            work(own[side], blocks[slot], acc.at[side], loss.at[side], scale, bias)
+
+        @pl.when(slot == SECOND)
+        def _():
+            each(lambda index: to_near(index).wait_recv(), 0, PARTS - 1)
+            work(own[core], second[0:rows - part], acc.at[core], loss.at[core], scale, bias)
+
+        @pl.when(phase == 0)
+        def _():
+            @pl.when(early_images)
+            def _():
+                pass_on()
+
+            follow()
+
         return carry
 
-    lax.fori_loop(PARTNER, SECOND, visit, 0)
-
-    to_near(0).wait_recv()
-    to_near(1).wait_recv()
-    half = rows // 2
-    work(own[core], second[0:half], acc.at[core], loss.at[core], scale, bias)
-    to_near(2).wait_recv()
-    work(own[core], second[half:half + part], acc.at[core], loss.at[core], scale, bias)
+    lax.fori_loop(0, 4, visit, 0)
 
     def drain(index):
         to_partner(own.at[1 - core], index).wait_send()
@@ -161,7 +183,7 @@
         relay(index).wait_send()
 
     each(drain)
-    to_near(3).wait_recv()
+    to_near(PARTS - 1).wait_recv()
 
 
 def finish_kernel(acc, loss, own, second, scale_ref, bias_ref, loss_ref, image_ref, text_ref, row_loss, sems):

time: 36.1 us -> 35.5 us (0.983)
  the two profiles are of different devices: /device:TPU:1 before, /device:TPU:6 now
where the time goes in v4:
time: 35.5 us; the launch traced here: 35.3 us
  Pallas kernels  33.4 us (94%)
  between operations  1.93 us (5%)
    pallas_call x1, Pallas kernels, body(): pl.pallas_call(functools.partial(ring_kernel, devices), out_shape=(pltpu....  31.5 us
    pallas_call x1, Pallas kernels, body(): pl.pallas_call(finish_kernel, out_shape=(jax.ShapeDtypeStruct((1, rows),...  1.87 us

profile of v4, /device:TPU:6, one launch (start us, length us, event | category | flops | bytes accessed | tf_op | source)
XLA Modules:
  0.0 35.3 jit_solution(16303523615974082793)
XLA Ops:
  1.9 31.5 %sigmoid_ring.1 = (f32[2,512,768]{2,1,0:T(8,128)S(1)}, f32[2,512,128]{2,1,0:T(8,128)S(1)}, bf16[2,512,768]{2,1,0:T(8,128)(2,1)S(1)}, bf16[512,768]{1,0:T(8,128)(2,1)S(1)}) custom-call(bf16[512,768]{1,0:T(8,128)(2,1)} %image_ref.1, bf16[512,768]{1,0:T(8,128)(2,1)} %text_ref.1, f32[1]{0:T(128)S(6)} %copy.7.scale_ref, f32[1]{0:T(128)S(6)} %copy.8.bias_ref), custom_call_target="tpu_custom_call" | custom-call | tf_op jit(solution)/shard_map/sigmoid_ring/pallas_call | solution.py:236
  33.5 1.9 %finish.1 = (f32[1,512]{1,0:T(1,128)}, f32[512,768]{1,0:T(8,128)}, f32[512,768]{1,0:T(8,128)}) custom-call(f32[2,512,768]{2,1,0:T(8,128)S(1)} %get-tuple-element.10.acc, f32[2,512,128]{2,1,0:T(8,128)S(1)} %get-tuple-element.11.loss, bf16[2,512,768]{2,1,0:T(8,128)(2,1)S(1)} %get-tuple-element.12.own, bf16[512,768]{1,0:T(8,128)(2,1)S(1)} %get-tuple-element.13.second, ...), custom_call_target="tpu_custom_call" | custom-call | tf_op jit(solution)/shard_map/finish/pallas_call | solution.py:259

commit v5 on v4

--- a/solution.py
+++ b/solution.py
@@ -10,7 +10,8 @@
 MESH = pl.DeviceIdType.MESH
 PARTS = 4
 TILES = 4
-HEIGHT, DEPTH = 4, 16
+WIDTH, HEIGHT, DEPTH = 4, 4, 16
+HELP = 32
 NT = (((1,), (1,)), ((), ()))
 PARTNER, DIRECT, RELAYED, SECOND = 0, 1, 2, 3
 
@@ -40,7 +41,8 @@
 
 
 def ring_kernel(devices, image_ref, text_ref, scale_ref, bias_ref, acc, loss, own, second,
-                blocks, load_sem, send, recv, here, ready):
+                blocks, extra, load_sem, send, recv, here, helpers_in, help_ok,
+                help_send, help_recv, lift_send, lift_recv):
     me = lax.axis_index("dp")
     core = lax.rem(me, 2)
     step = 2 * core - 1
@@ -50,13 +52,83 @@
     rows = own.shape[1]
     part = rows // PARTS
 
+    chip = lax.div(me, 2)
+    z = lax.rem(chip, DEPTH)
+    y = lax.rem(lax.div(chip, DEPTH), HEIGHT)
+    x = lax.div(chip, DEPTH * HEIGHT)
+    starts = z == 0
+    corner = y == 0
+
     barrier = pltpu.get_barrier_semaphore()
-    previous = lax.rem(me - 1 - core + devices, devices)
-    pl.semaphore_signal(barrier, inc=1, device_id=(previous,), device_id_type=MESH)
+
+    def greet(distance):
+        pl.semaphore_signal(
+            barrier, inc=1, device_id=(lax.rem(me + distance + devices, devices),), device_id_type=MESH)
+
+    greet(-1 - core)
+    greet(2 - core)
 
     @pl.when(core == 1)
     def _():
-        pl.semaphore_signal(barrier, inc=1, device_id=(partner,), device_id_type=MESH)
+        greet(-1)
+
+    helpers = HEIGHT - 1
+    ends = z == DEPTH - 1
+    before = x != WIDTH - 1
+    after = x != 0
+    up_pole = jnp.logical_and(jnp.logical_and(ends, before), jnp.logical_and(y == helpers, core == 1))
+    up_helper = jnp.logical_and(jnp.logical_and(ends, after), jnp.logical_and(y != helpers, core == 1))
+    down_pole = jnp.logical_and(jnp.logical_and(starts, after), jnp.logical_and(corner, core == 0))
+    down_helper = jnp.logical_and(jnp.logical_and(starts, before), jnp.logical_and(y != 0, core == 0))
+    pole = jnp.logical_or(up_pole, down_pole)
+    helper = jnp.logical_or(up_helper, down_helper)
+    helper_line = y - 1 + core
+
+    def device_at(x, y, z, core):
+        return 2 * ((x * HEIGHT + y) * DEPTH + z) + core
+
+    def up_helper_at(x, line):
+        return device_at(x, line, DEPTH - 1, 1)
+
+    def down_helper_at(x, line):
+        return device_at(x, line + 1, 0, 0)
+
+    up_pole_here = device_at(x, helpers, DEPTH - 1, 1)
+    down_pole_here = device_at(x, 0, 0, 0)
+    next_x = lax.rem(x + 1, WIDTH)
+    last_x = lax.rem(x + WIDTH - 1, WIDTH)
+
+    def tell(semaphore, device):
+        pl.semaphore_signal(semaphore, inc=1, device_id=(device,), device_id_type=MESH)
+
+    @pl.when(down_pole)
+    def _():
+        for line in range(helpers):
+            tell(barrier, up_helper_at(x, line))
+
+    @pl.when(down_helper)
+    def _():
+        tell(barrier, device_at(next_x, 0, 0, 0))
+
+    def help_rows(line):
+        return pl.ds(pl.multiple_of(rows - HELP * (helpers - line), HELP), HELP)
+
+    def ask(line):
+        device = jnp.where(core == 1, up_helper_at(next_x, line), down_helper_at(last_x, line))
+        return pltpu.make_async_remote_copy(
+            src_ref=blocks.at[PARTNER, help_rows(line)], dst_ref=extra, send_sem=help_send.at[line],
+            recv_sem=help_recv, device_id=(device,), device_id_type=MESH)
+
+    def lift(line):
+        return pltpu.make_async_remote_copy(
+            src_ref=extra, dst_ref=second.at[help_rows(line)], send_sem=lift_send, recv_sem=lift_recv.at[line],
+            device_id=(jnp.where(core == 1, down_pole_here, up_pole_here),), device_id_type=MESH)
+
+    def short():
+        piece = pl.ds(rows - part, part - HELP * helpers)
+        return pltpu.make_async_remote_copy(
+            src_ref=blocks.at[PARTNER, piece], dst_ref=second.at[piece], send_sem=send.at[SECOND, PARTS - 1],
+            recv_sem=recv.at[SECOND, PARTS - 1], device_id=(near,), device_id_type=MESH)
 
     loads = [
         pltpu.make_async_copy(source, target, load_sem.at[slot])
@@ -91,26 +163,42 @@
             return carry
         lax.fori_loop(first, last, run, 0)
 
+    def start_zero():
+        pl.semaphore_wait(barrier, jnp.where(down_pole, 3 + helpers, 3))
+        pl.semaphore_signal(here, inc=1, device_id=(partner,), device_id_type=MESH)
+        each(lambda index: to_far(image_ref, index).start())
+        each(lambda index: to_partner(text_ref, index).start())
+
+        @pl.when(down_pole)
+        def _():
+            for line in range(helpers):
+                tell(help_ok, down_helper_at(last_x, line))
+            pl.semaphore_wait(helpers_in, helpers)
+            tell(help_ok, lax.rem(me - 1 + devices, devices))
+
+    def start_one():
+        pl.semaphore_wait(here, 1)
+        each(lambda index: to_partner(image_ref, index).start())
+
+    def when(core_is, starts_is, action):
+        @pl.when(jnp.logical_and(core == core_is, starts if starts_is else jnp.logical_not(starts)))
+        def _():
+            action()
+
     @pl.when(core == 1)
     def _():
-        pl.semaphore_wait(barrier, 2)
+        pl.semaphore_wait(barrier, jnp.where(up_helper, 3, 2))
         each(lambda index: to_far(text_ref, index).start())
-        pl.semaphore_wait(here, 1)
-        pl.semaphore_signal(ready, inc=1, device_id=(near,), device_id_type=MESH)
-        each(lambda index: to_partner(image_ref, index).start())
-        for load in loads:
-            load.start()
-
-    @pl.when(core == 0)
-    def _():
-        pl.semaphore_wait(barrier, 1)
-        pl.semaphore_signal(here, inc=1, device_id=(partner,), device_id_type=MESH)
-        each(lambda index: to_partner(text_ref, index).start())
-        for load in loads:
-            load.start()
-        pl.semaphore_wait(ready, 1)
-        each(lambda index: to_far(image_ref, index).start())
-
+
+        @pl.when(up_helper)
+        def _():
+            tell(helpers_in, down_pole_here)
+
+    for load in loads:
+        load.start()
+
+    when(0, False, start_zero)
+    when(1, False, start_one)
     for load in loads:
         load.wait()
     scale = scale_ref[0]
@@ -123,23 +211,56 @@
 
     def follow():
         each(lambda index: to_far(own.at[core], index).wait_send(), 0, PARTS - 1)
+
+        @pl.when(up_pole)
+        def _():
+            pl.semaphore_wait(help_ok, 1)
+
+        @pl.when(pole)
+        def _():
+            for line in range(helpers):
+                ask(line).start()
+
         to_near(0).start()
         to_far(own.at[core], PARTS - 1).wait_send()
-        each(lambda index: to_near(index).start(), 1)
-
-    def pass_on():
+        each(lambda index: to_near(index).start(), 1, PARTS - 1)
+
+        @pl.when(pole)
+        def _():
+            short().start()
+
+        @pl.when(jnp.logical_not(jnp.logical_or(pole, up_helper)))
+        def _():
+            to_near(PARTS - 1).start()
+
+    def carry_over():
+        ask(helper_line).wait_recv()
+        lift(helper_line).start()
+
+    def pass_on(first=0, last=PARTS):
         def run(index):
             to_far(own.at[core], index).wait_recv()
             relay(index).start()
-        each(run)
-
-    chip = lax.div(me, 2)
-    starts = lax.rem(chip, DEPTH) == 0
-    corner = lax.rem(lax.div(chip, DEPTH), HEIGHT) == 0
+        each(run, first, last)
+
     early_images = jnp.logical_and(starts, core == 0)
     late_texts = jnp.logical_and(starts, core == 1)
+    late_corner = jnp.logical_and(late_texts, corner)
+
+    when(0, True, start_zero)
+    when(1, True, start_one)
 
     def visit(phase, carry):
+        @pl.when(jnp.logical_and(up_helper, phase == 1))
+        def _():
+            carry_over()
+            to_near(PARTS - 1).start()
+
+        @pl.when(jnp.logical_and(down_helper, phase == 2))
+        def _():
+            pl.semaphore_wait(help_ok, 1)
+            carry_over()
+
         slot = jnp.where(late_texts, jnp.where(phase == PARTNER, PARTNER, jnp.where(
             phase == 1, RELAYED, jnp.where((phase == 2) == corner, SECOND, DIRECT))), phase)
 
@@ -149,7 +270,7 @@
 
         @pl.when(jnp.logical_and(slot == DIRECT, jnp.logical_not(early_images)))
         def _():
-            pass_on()
+            pass_on(jnp.where(late_corner, PARTS // 2, 0))
 
         @pl.when(slot == RELAYED)
         def _():
@@ -162,6 +283,10 @@
 
         @pl.when(slot == SECOND)
         def _():
+            @pl.when(late_corner)
+            def _():
+                pass_on(0, PARTS // 2)
+
             each(lambda index: to_near(index).wait_recv(), 0, PARTS - 1)
             work(own[core], second[0:rows - part], acc.at[core], loss.at[core], scale, bias)
 
@@ -179,11 +304,34 @@
 
     def drain(index):
         to_partner(own.at[1 - core], index).wait_send()
-        to_near(index).wait_send()
         relay(index).wait_send()
 
     each(drain)
-    to_near(PARTS - 1).wait_recv()
+    each(lambda index: to_near(index).wait_send(), 0, PARTS - 1)
+
+    @pl.when(pole)
+    def _():
+        short().wait_send()
+        for line in range(helpers):
+            ask(line).wait_send()
+
+    @pl.when(jnp.logical_not(pole))
+    def _():
+        to_near(PARTS - 1).wait_send()
+
+    @pl.when(helper)
+    def _():
+        lift(helper_line).wait_send()
+
+    @pl.when(pole)
+    def _():
+        for line in range(helpers):
+            lift(line).wait_recv()
+        short().wait_recv()
+
+    @pl.when(jnp.logical_not(pole))
+    def _():
+        to_near(PARTS - 1).wait_recv()
 
 
 def finish_kernel(acc, loss, own, second, scale_ref, bias_ref, loss_ref, image_ref, text_ref, row_loss, sems):
@@ -245,11 +393,17 @@
         out_specs=(vmem, vmem, vmem, vmem),
         scratch_shapes=[
             pltpu.VMEM((3, rows, width), jnp.bfloat16),
+            pltpu.VMEM((HELP, width), jnp.bfloat16),
             pltpu.SemaphoreType.DMA((2,)),
             pltpu.SemaphoreType.DMA((4, PARTS)),
             pltpu.SemaphoreType.DMA((4, PARTS)),
             pltpu.SemaphoreType.REGULAR,
             pltpu.SemaphoreType.REGULAR,
+            pltpu.SemaphoreType.REGULAR,
+            pltpu.SemaphoreType.DMA((HEIGHT - 1,)),
+            pltpu.SemaphoreType.DMA,
+            pltpu.SemaphoreType.DMA,
+            pltpu.SemaphoreType.DMA((HEIGHT - 1,)),
         ],
         compiler_params=pltpu.CompilerParams(
             collective_id=0, has_side_effects=True, vmem_limit_bytes=32 << 20),

time: 35.5 us -> 34.7 us (0.977)
  Pallas kernels: 33.4 us -> 32.6 us
    pallas_call x1, Pallas kernels: 31.5 us -> 30.7 us  [body(): pl.pallas_call(functools.partial(ring_kernel, devices), out_shape=(pltpu....]
where the time goes in v5:
time: 34.7 us; the launch traced here: 34.5 us
  Pallas kernels  32.6 us (94%)
  between operations  1.93 us (6%)
    pallas_call x1, Pallas kernels, body(): pl.pallas_call(functools.partial(ring_kernel, devices), out_shape=(pltpu....  30.7 us
    pallas_call x1, Pallas kernels, body(): pl.pallas_call(finish_kernel, out_shape=(jax.ShapeDtypeStruct((1, rows),...  1.87 us

profile of v5, /device:TPU:6, one launch (start us, length us, event | category | flops | bytes accessed | tf_op | source)
XLA Modules:
  0.0 34.5 jit_solution(3044414281275349441)
XLA Ops:
  1.9 30.7 %sigmoid_ring.1 = (f32[2,512,768]{2,1,0:T(8,128)S(1)}, f32[2,512,128]{2,1,0:T(8,128)S(1)}, bf16[2,512,768]{2,1,0:T(8,128)(2,1)S(1)}, bf16[512,768]{1,0:T(8,128)(2,1)S(1)}) custom-call(bf16[512,768]{1,0:T(8,128)(2,1)} %image_ref.1, bf16[512,768]{1,0:T(8,128)(2,1)} %text_ref.1, f32[1]{0:T(128)S(6)} %copy.7.scale_ref, f32[1]{0:T(128)S(6)} %copy.8.bias_ref), custom_call_target="tpu_custom_call" | custom-call | tf_op jit(solution)/shard_map/sigmoid_ring/pallas_call | solution.py:384
  32.7 1.9 %finish.1 = (f32[1,512]{1,0:T(1,128)}, f32[512,768]{1,0:T(8,128)}, f32[512,768]{1,0:T(8,128)}) custom-call(f32[2,512,768]{2,1,0:T(8,128)S(1)} %get-tuple-element.10.acc, f32[2,512,128]{2,1,0:T(8,128)S(1)} %get-tuple-element.11.loss, bf16[2,512,768]{2,1,0:T(8,128)(2,1)S(1)} %get-tuple-element.12.own, bf16[512,768]{1,0:T(8,128)(2,1)S(1)} %get-tuple-element.13.second, ...), custom_call_target="tpu_custom_call" | custom-call | tf_op jit(solution)/shard_map/finish/pallas_call | solution.py:413

commit v6 on v5

--- a/solution.py
+++ b/solution.py
@@ -11,7 +11,7 @@
 PARTS = 4
 TILES = 4
 WIDTH, HEIGHT, DEPTH = 4, 4, 16
-HELP = 32
+HELP = (48, 32, 16)
 NT = (((1,), (1,)), ((), ()))
 PARTNER, DIRECT, RELAYED, SECOND = 0, 1, 2, 3
 
@@ -111,21 +111,28 @@
         tell(barrier, device_at(next_x, 0, 0, 0))
 
     def help_rows(line):
-        return pl.ds(pl.multiple_of(rows - HELP * (helpers - line), HELP), HELP)
+        return pl.ds(rows - sum(HELP[line:]), HELP[line])
 
     def ask(line):
         device = jnp.where(core == 1, up_helper_at(next_x, line), down_helper_at(last_x, line))
         return pltpu.make_async_remote_copy(
-            src_ref=blocks.at[PARTNER, help_rows(line)], dst_ref=extra, send_sem=help_send.at[line],
-            recv_sem=help_recv, device_id=(device,), device_id_type=MESH)
+            src_ref=blocks.at[PARTNER, help_rows(line)], dst_ref=extra.at[pl.ds(0, HELP[line])],
+            send_sem=help_send.at[line], recv_sem=help_recv, device_id=(device,), device_id_type=MESH)
 
     def lift(line):
         return pltpu.make_async_remote_copy(
-            src_ref=extra, dst_ref=second.at[help_rows(line)], send_sem=lift_send, recv_sem=lift_recv.at[line],
-            device_id=(jnp.where(core == 1, down_pole_here, up_pole_here),), device_id_type=MESH)
+            src_ref=extra.at[pl.ds(0, HELP[line])], dst_ref=second.at[help_rows(line)], send_sem=lift_send,
+            recv_sem=lift_recv.at[line], device_id=(jnp.where(core == 1, down_pole_here, up_pole_here),),
+            device_id_type=MESH)
+
+    def on_line(action):
+        for line in range(helpers):
+            @pl.when(helper_line == line)
+            def _():
+                action(line)
 
     def short():
-        piece = pl.ds(rows - part, part - HELP * helpers)
+        piece = pl.ds(rows - part, part - sum(HELP))
         return pltpu.make_async_remote_copy(
             src_ref=blocks.at[PARTNER, piece], dst_ref=second.at[piece], send_sem=send.at[SECOND, PARTS - 1],
             recv_sem=recv.at[SECOND, PARTS - 1], device_id=(near,), device_id_type=MESH)
@@ -234,8 +241,11 @@
             to_near(PARTS - 1).start()
 
     def carry_over():
-        ask(helper_line).wait_recv()
-        lift(helper_line).start()
+        def run(line):
+            ask(line).wait_recv()
+            lift(line).start()
+
+        on_line(run)
 
     def pass_on(first=0, last=PARTS):
         def run(index):
@@ -256,7 +266,7 @@
             carry_over()
             to_near(PARTS - 1).start()
 
-        @pl.when(jnp.logical_and(down_helper, phase == 2))
+        @pl.when(jnp.logical_and(down_helper, phase == 3))
         def _():
             pl.semaphore_wait(help_ok, 1)
             carry_over()
@@ -287,8 +297,11 @@
             def _():
                 pass_on(0, PARTS // 2)
 
-            each(lambda index: to_near(index).wait_recv(), 0, PARTS - 1)
-            work(own[core], second[0:rows - part], acc.at[core], loss.at[core], scale, bias)
+            half = rows // 2
+            each(lambda index: to_near(index).wait_recv(), 0, PARTS // 2)
+            work(own[core], second[0:half], acc.at[core], loss.at[core], scale, bias)
+            to_near(PARTS // 2).wait_recv()
+            work(own[core], second[half:half + part], acc.at[core], loss.at[core], scale, bias)
 
         @pl.when(phase == 0)
         def _():
@@ -321,7 +334,7 @@
 
     @pl.when(helper)
     def _():
-        lift(helper_line).wait_send()
+        on_line(lambda line: lift(line).wait_send())
 
     @pl.when(pole)
     def _():
@@ -393,7 +406,7 @@
         out_specs=(vmem, vmem, vmem, vmem),
         scratch_shapes=[
             pltpu.VMEM((3, rows, width), jnp.bfloat16),
-            pltpu.VMEM((HELP, width), jnp.bfloat16),
+            pltpu.VMEM((max(HELP), width), jnp.bfloat16),
             pltpu.SemaphoreType.DMA((2,)),
             pltpu.SemaphoreType.DMA((4, PARTS)),
             pltpu.SemaphoreType.DMA((4, PARTS)),

time: 34.7 us -> 34.1 us (0.983)
  Pallas kernels: 32.6 us -> 32 us
    pallas_call x1, Pallas kernels: 30.7 us -> 30.1 us  [body(): pl.pallas_call(functools.partial(ring_kernel, devices), out_shape=(pltpu....]
where the time goes in v6:
time: 34.1 us; the launch traced here: 33.9 us
  Pallas kernels  32 us (94%)
  between operations  1.93 us (6%)
    pallas_call x1, Pallas kernels, body(): pl.pallas_call(functools.partial(ring_kernel, devices), out_shape=(pltpu....  30.1 us
    pallas_call x1, Pallas kernels, body(): pl.pallas_call(finish_kernel, out_shape=(jax.ShapeDtypeStruct((1, rows),...  1.87 us

profile of v6, /device:TPU:6, one launch (start us, length us, event | category | flops | bytes accessed | tf_op | source)
XLA Modules:
  0.0 33.9 jit_solution(16581029157070490321)
XLA Ops:
  1.9 30.1 %sigmoid_ring.1 = (f32[2,512,768]{2,1,0:T(8,128)S(1)}, f32[2,512,128]{2,1,0:T(8,128)S(1)}, bf16[2,512,768]{2,1,0:T(8,128)(2,1)S(1)}, bf16[512,768]{1,0:T(8,128)(2,1)S(1)}) custom-call(bf16[512,768]{1,0:T(8,128)(2,1)} %image_ref.1, bf16[512,768]{1,0:T(8,128)(2,1)} %text_ref.1, f32[1]{0:T(128)S(6)} %copy.7.scale_ref, f32[1]{0:T(128)S(6)} %copy.8.bias_ref), custom_call_target="tpu_custom_call" | custom-call | tf_op jit(solution)/shard_map/sigmoid_ring/pallas_call | solution.py:397
  32.0 1.9 %finish.1 = (f32[1,512]{1,0:T(1,128)}, f32[512,768]{1,0:T(8,128)}, f32[512,768]{1,0:T(8,128)}) custom-call(f32[2,512,768]{2,1,0:T(8,128)S(1)} %get-tuple-element.10.acc, f32[2,512,128]{2,1,0:T(8,128)S(1)} %get-tuple-element.11.loss, bf16[2,512,768]{2,1,0:T(8,128)(2,1)S(1)} %get-tuple-element.12.own, bf16[512,768]{1,0:T(8,128)(2,1)S(1)} %get-tuple-element.13.second, ...), custom_call_target="tpu_custom_call" | custom-call | tf_op jit(solution)/shard_map/finish/pallas_call | solution.py:426

commit v7 on v6

--- a/solution.py
+++ b/solution.py
@@ -65,8 +65,8 @@
         pl.semaphore_signal(
             barrier, inc=1, device_id=(lax.rem(me + distance + devices, devices),), device_id_type=MESH)
 
+    greet(2 - core)
     greet(-1 - core)
-    greet(2 - core)
 
     @pl.when(core == 1)
     def _():
@@ -170,11 +170,11 @@
             return carry
         lax.fori_loop(first, last, run, 0)
 
-    def start_zero():
+    def start_zero(images, texts):
         pl.semaphore_wait(barrier, jnp.where(down_pole, 3 + helpers, 3))
         pl.semaphore_signal(here, inc=1, device_id=(partner,), device_id_type=MESH)
-        each(lambda index: to_far(image_ref, index).start())
-        each(lambda index: to_partner(text_ref, index).start())
+        each(lambda index: to_far(images, index).start())
+        each(lambda index: to_partner(texts, index).start())
 
         @pl.when(down_pole)
         def _():
@@ -204,7 +204,7 @@
     for load in loads:
         load.start()
 
-    when(0, False, start_zero)
+    when(0, False, lambda: start_zero(image_ref, text_ref))
     when(1, False, start_one)
     for load in loads:
         load.wait()
@@ -257,7 +257,7 @@
     late_texts = jnp.logical_and(starts, core == 1)
     late_corner = jnp.logical_and(late_texts, corner)
 
-    when(0, True, start_zero)
+    when(0, True, lambda: start_zero(own.at[0], own.at[1]))
     when(1, True, start_one)
 
     def visit(phase, carry):

time: 34.1 us -> 34.1 us (level)
  no operation moved by 1% of the time
where the time goes in v7:
time: 34.1 us; the launch traced here: 33.9 us
  Pallas kernels  32 us (94%)
  between operations  1.93 us (6%)
    pallas_call x1, Pallas kernels, body(): pl.pallas_call(functools.partial(ring_kernel, devices), out_shape=(pltpu....  30.1 us
    pallas_call x1, Pallas kernels, body(): pl.pallas_call(finish_kernel, out_shape=(jax.ShapeDtypeStruct((1, rows),...  1.87 us

profile of v7, /device:TPU:6, one launch (start us, length us, event | category | flops | bytes accessed | tf_op | source)
XLA Modules:
  0.0 33.9 jit_solution(9699953132917838091)
XLA Ops:
  1.9 30.1 %sigmoid_ring.1 = (f32[2,512,768]{2,1,0:T(8,128)S(1)}, f32[2,512,128]{2,1,0:T(8,128)S(1)}, bf16[2,512,768]{2,1,0:T(8,128)(2,1)S(1)}, bf16[512,768]{1,0:T(8,128)(2,1)S(1)}) custom-call(bf16[512,768]{1,0:T(8,128)(2,1)} %image_ref.1, bf16[512,768]{1,0:T(8,128)(2,1)} %text_ref.1, f32[1]{0:T(128)S(6)} %copy.7.scale_ref, f32[1]{0:T(128)S(6)} %copy.8.bias_ref), custom_call_target="tpu_custom_call" | custom-call | tf_op jit(solution)/shard_map/sigmoid_ring/pallas_call | solution.py:397
  32.0 1.9 %finish.1 = (f32[1,512]{1,0:T(1,128)}, f32[512,768]{1,0:T(8,128)}, f32[512,768]{1,0:T(8,128)}) custom-call(f32[2,512,768]{2,1,0:T(8,128)S(1)} %get-tuple-element.10.acc, f32[2,512,128]{2,1,0:T(8,128)S(1)} %get-tuple-element.11.loss, bf16[2,512,768]{2,1,0:T(8,128)(2,1)S(1)} %get-tuple-element.12.own, bf16[512,768]{1,0:T(8,128)(2,1)S(1)} %get-tuple-element.13.second, ...), custom_call_target="tpu_custom_call" | custom-call | tf_op jit(solution)/shard_map/finish/pallas_call | solution.py:426

commit v8 on v7

--- a/solution.py
+++ b/solution.py
@@ -11,7 +11,7 @@
 PARTS = 4
 TILES = 4
 WIDTH, HEIGHT, DEPTH = 4, 4, 16
-HELP = (48, 32, 16)
+HELP = (64, 16, 16)
 NT = (((1,), (1,)), ((), ()))
 PARTNER, DIRECT, RELAYED, SECOND = 0, 1, 2, 3
 
@@ -82,7 +82,7 @@
     down_helper = jnp.logical_and(jnp.logical_and(starts, before), jnp.logical_and(y != 0, core == 0))
     pole = jnp.logical_or(up_pole, down_pole)
     helper = jnp.logical_or(up_helper, down_helper)
-    helper_line = y - 1 + core
+    helper_line = jnp.where(core == 1, y, helpers - y)
 
     def device_at(x, y, z, core):
         return 2 * ((x * HEIGHT + y) * DEPTH + z) + core
@@ -91,7 +91,7 @@
         return device_at(x, line, DEPTH - 1, 1)
 
     def down_helper_at(x, line):
-        return device_at(x, line + 1, 0, 0)
+        return device_at(x, helpers - line, 0, 0)
 
     up_pole_here = device_at(x, helpers, DEPTH - 1, 1)
     down_pole_here = device_at(x, 0, 0, 0)

time: 34.1 us -> 34.2 us (level)
  no operation moved by 1% of the time
where the time goes in v8:
time: 34.2 us; the launch traced here: 33.9 us
  Pallas kernels  32 us (94%)
  between operations  1.93 us (6%)
    pallas_call x1, Pallas kernels, body(): pl.pallas_call(functools.partial(ring_kernel, devices), out_shape=(pltpu....  30.1 us
    pallas_call x1, Pallas kernels, body(): pl.pallas_call(finish_kernel, out_shape=(jax.ShapeDtypeStruct((1, rows),...  1.87 us

profile of v8, /device:TPU:6, one launch (start us, length us, event | category | flops | bytes accessed | tf_op | source)
XLA Modules:
  0.0 33.9 jit_solution(14960571670159922596)
XLA Ops:
  1.9 30.1 %sigmoid_ring.1 = (f32[2,512,768]{2,1,0:T(8,128)S(1)}, f32[2,512,128]{2,1,0:T(8,128)S(1)}, bf16[2,512,768]{2,1,0:T(8,128)(2,1)S(1)}, bf16[512,768]{1,0:T(8,128)(2,1)S(1)}) custom-call(bf16[512,768]{1,0:T(8,128)(2,1)} %image_ref.1, bf16[512,768]{1,0:T(8,128)(2,1)} %text_ref.1, f32[1]{0:T(128)S(6)} %copy.7.scale_ref, f32[1]{0:T(128)S(6)} %copy.8.bias_ref), custom_call_target="tpu_custom_call" | custom-call | tf_op jit(solution)/shard_map/sigmoid_ring/pallas_call | solution.py:397
  32.0 1.9 %finish.1 = (f32[1,512]{1,0:T(1,128)}, f32[512,768]{1,0:T(8,128)}, f32[512,768]{1,0:T(8,128)}) custom-call(f32[2,512,768]{2,1,0:T(8,128)S(1)} %get-tuple-element.10.acc, f32[2,512,128]{2,1,0:T(8,128)S(1)} %get-tuple-element.11.loss, bf16[2,512,768]{2,1,0:T(8,128)(2,1)S(1)} %get-tuple-element.12.own, bf16[512,768]{1,0:T(8,128)(2,1)S(1)} %get-tuple-element.13.second, ...), custom_call_target="tpu_custom_call" | custom-call | tf_op jit(solution)/shard_map/finish/pallas_call | solution.py:426
